TPU v7x, 32 devices: a whole 2x2x4 slice. The times are simulated.
32 devices in a mesh: dp: 4 (over x, core), seq: 8 (over z, y).
Axes of the slice: x: 2, y: 2, z: 4, core: 2. Of those that a mesh axis runs over, the one named last changes fastest.
Arguments:
- activations: bfloat16 [16384, 1280], P(('dp', 'seq')), may hold values from -6 to 6
- cotangent: bfloat16 [16384, 1280], P(('dp', 'seq')), may hold values from -6 to 6
- w_proj: bfloat16 [1280, 256], P(('dp', 'seq')), may hold values from -0.15625 to 0.15625
- forward_decay: float32 [16384, 20], P(('dp', 'seq')), may hold values from -1 to 0
- reverse_decay: float32 [16384, 20], P(('dp', 'seq')), may hold values from -1 to 0
- forward_state: bfloat16 [32, 64, 1280], P(('dp', 'seq')), may hold values from -6 to 6
- reverse_state: bfloat16 [32, 64, 1280], P(('dp', 'seq')), may hold values from -6 to 6
Outputs:
- grad_inputs: bfloat16 [16384, 1280], P(('dp', 'seq'))
- grad_weight: float32 [1280, 256], P(('dp', 'seq'))
- grad_forward_decay: float32 [16384, 20], P(('dp', 'seq'))
- grad_reverse_decay: float32 [16384, 20], P(('dp', 'seq'))
All inputs are finite; a program needn't handle non-finite values.
Results may differ from a plain program's by a relative error of at most 0.0085.
Values may be sent and summed in bfloat16 or wider, within the bound.
A program may use at most 192 MiB of HBM per device.

v0:
```python
import jax
import jax.numpy as jnp
from jax import lax
from jax.sharding import PartitionSpec as P


def carried_in(x, axis, combine, identity):
    count, here = (lax.axis_size(axis), lax.axis_index(axis))
    everything = jax.tree.map(lambda part: lax.all_gather(part, axis), x)
    start = jax.tree.map(
        lambda part, zero: jnp.broadcast_to(jnp.asarray(zero, part.dtype), part.shape), x, identity
    )

    def hop(k, before):
        at = count - 1 - k
        reached = at > here
        new = combine(before, jax.tree.map(lambda part: part[at], everything))
        return jax.tree.map(lambda a, b: jnp.where(reached, a, b), new, before)

    return lax.fori_loop(0, count, hop, start)


def entering(x, axis, join, neutral):
    place = lax.axis_index(axis)
    gathered = jax.tree.map(
        lambda a, kind: lax.all_gather(a.astype(kind), axis), x, (jnp.bfloat16, jnp.bfloat16)
    )
    state = jax.tree.map(lambda a, e: jnp.zeros_like(a) + jnp.asarray(e, a.dtype), x, neutral)

    def one(hop, state):
        return join(
            state,
            jax.tree.map(
                lambda a, own: lax.dynamic_index_in_dim(a, hop, 0, False).astype(own.dtype),
                gathered,
                x,
            ),
        )

    return lax.fori_loop(0, place, one, state)


def head_columns(values, head_size):
    return jnp.repeat(values, head_size, axis=-1)


def head_sums(values, head_count):
    return values.reshape(values.shape[:-1] + (head_count, values.shape[-1] // head_count)).sum(-1)


def intra_terms(in_rows, cot_rows, b_rows, c_rows, decays):
    length, head_count = decays.shape
    head_size = in_rows.shape[1] // head_count
    group_size = 4
    scaling = b_rows.shape[1] ** (-0.5)
    cumulative = jnp.cumsum(decays, axis=0)
    scores = jnp.dot(b_rows, c_rows.T, preferred_element_type=jnp.float32)
    positions = jnp.arange(length)
    upper_mask = positions[:, None] <= positions[None, :]
    in_heads = in_rows.reshape(length, head_count, head_size)
    cot_heads = cot_rows.reshape(length, head_count, head_size)

    def one_group(group_index):
        first_head = group_index * group_size
        in_group = lax.dynamic_slice_in_dim(in_heads, first_head, group_size, 1)
        cot_group = lax.dynamic_slice_in_dim(cot_heads, first_head, group_size, 1)
        cum_group = lax.dynamic_slice_in_dim(cumulative, first_head, group_size, 1)
        exponent = cum_group.T[:, None, :] - cum_group.T[:, :, None]
        decay_mat = jnp.where(upper_mask, jnp.exp(jnp.where(upper_mask, exponent, 0.0)), 0.0)
        products = jnp.einsum(
            "thp,uhp->htu", in_group, cot_group, preferred_element_type=jnp.float32
        )
        weighted = scaling * scores[None] * decay_mat
        mixing_part = jnp.sum(decay_mat * products, axis=0)
        grad_group = jnp.einsum(
            "htu,uhp->thp",
            weighted.astype(jnp.bfloat16),
            cot_group,
            preferred_element_type=jnp.float32,
        )
        pair_terms = weighted * products
        increment = pair_terms.sum(2) - pair_terms.sum(1)
        return (grad_group, mixing_part, jnp.cumsum(increment, axis=1) - increment)

    grad_groups, mixing_parts, decay_groups = lax.map(
        one_group, jnp.arange(head_count // group_size)
    )
    grad_in = jnp.moveaxis(grad_groups, 0, 1).reshape(length, -1)
    mixing_low = jnp.sum(mixing_parts, axis=0).astype(jnp.bfloat16)
    grad_decay = decay_groups.reshape(head_count, length).T
    grad_b = scaling * jnp.dot(mixing_low, c_rows, preferred_element_type=jnp.float32)
    grad_c = scaling * jnp.dot(mixing_low.T, b_rows, preferred_element_type=jnp.float32)
    return (grad_in, grad_b, grad_c, grad_decay)


def cross_terms(in_rows, cot_rows, b_rows, c_rows, decays, initial, carried_low):
    head_count = decays.shape[1]
    head_size = in_rows.shape[1] // head_count
    scaling = b_rows.shape[1] ** (-0.5)
    cumulative = jnp.cumsum(decays, axis=0)
    block_total = cumulative[-1]
    growth = jnp.exp(head_columns(cumulative, head_size))
    shrink = jnp.exp(head_columns(block_total[None, :] - cumulative, head_size))
    b_carried = jnp.dot(b_rows, carried_low, preferred_element_type=jnp.float32)
    c_initial = jnp.dot(c_rows, initial, preferred_element_type=jnp.float32)
    grad_in = shrink * b_carried
    scaled_in = in_rows.astype(jnp.float32) * shrink
    grad_b = jnp.dot(
        scaled_in.astype(jnp.bfloat16), carried_low.T, preferred_element_type=jnp.float32
    )
    scaled_cot = cot_rows.astype(jnp.float32) * growth
    grad_c = scaling * jnp.dot(
        scaled_cot.astype(jnp.bfloat16), initial.T, preferred_element_type=jnp.float32
    )
    start_terms = scaling * head_sums(scaled_cot * c_initial, head_count)
    carry_terms = head_sums(scaled_in * b_carried, head_count)
    whole_block = jnp.exp(block_total) * head_sums(
        jnp.sum(carried_low.astype(jnp.float32) * initial.astype(jnp.float32), axis=0), head_count
    )
    grad_decay = (
        jnp.cumsum(start_terms[::-1], axis=0)[::-1]
        + (jnp.cumsum(carry_terms, axis=0) - carry_terms)
        + whole_block[None, :]
    )
    return (grad_in, grad_b, grad_c, grad_decay)


def summary(cot_rows, c_rows, decays):
    head_size = cot_rows.shape[1] // decays.shape[1]
    scaling = c_rows.shape[1] ** (-0.5)
    cumulative = jnp.cumsum(decays, axis=0)
    growth = jnp.exp(head_columns(cumulative, head_size))
    scaled_cot = (cot_rows.astype(jnp.float32) * growth).astype(jnp.bfloat16)
    outgoing = scaling * jnp.dot(c_rows.T, scaled_cot, preferred_element_type=jnp.float32)
    return (jnp.exp(cumulative[-1]), outgoing)


def compose(earlier, later):
    head_size = earlier[1].shape[1] // earlier[0].shape[0]
    return (
        earlier[0] * later[0],
        head_columns(later[0], head_size)[None, :] * earlier[1] + later[1],
    )


def per_device(
    activations, cotangent, w_proj, forward_decay, reverse_decay, forward_state, reverse_state
):
    length, model_width = activations.shape
    head_count = forward_decay.shape[1]
    state_size = w_proj.shape[1] // 4
    all_weights = lax.all_gather(w_proj, ("dp", "seq"), axis=0, tiled=True)
    projected = jnp.dot(activations, all_weights, preferred_element_type=jnp.float32).astype(
        jnp.bfloat16
    )
    b_forward = projected[:, :state_size]
    c_forward = projected[:, state_size : 2 * state_size]
    flipped_in = activations[::-1]
    flipped_cot = cotangent[::-1]
    b_reverse = projected[::-1, 2 * state_size : 3 * state_size]
    c_reverse = projected[::-1, 3 * state_size :]
    decay_reverse = reverse_decay[::-1]
    factor_forward, outgoing_forward = summary(cotangent, c_forward, forward_decay)
    factor_reverse, outgoing_reverse = summary(flipped_cot, c_reverse, decay_reverse)
    neutral = (
        jnp.ones((head_count,), jnp.float32),
        jnp.zeros((state_size, model_width), jnp.float32),
    )
    carried_forward = carried_in((factor_forward, outgoing_forward), "seq", compose, neutral)[1]
    carried_reverse = entering((factor_reverse, outgoing_reverse), "seq", compose, neutral)[1]
    local_forward = intra_terms(activations, cotangent, b_forward, c_forward, forward_decay)
    local_reverse = intra_terms(flipped_in, flipped_cot, b_reverse, c_reverse, decay_reverse)
    remote_forward = cross_terms(
        activations,
        cotangent,
        b_forward,
        c_forward,
        forward_decay,
        forward_state[0],
        carried_forward.astype(jnp.bfloat16),
    )
    remote_reverse = cross_terms(
        flipped_in,
        flipped_cot,
        b_reverse,
        c_reverse,
        decay_reverse,
        reverse_state[0],
        carried_reverse.astype(jnp.bfloat16),
    )
    forward_parts = [
        near_term + far_term for near_term, far_term in zip(local_forward, remote_forward)
    ]
    reverse_parts = [
        (near_term + far_term)[::-1] for near_term, far_term in zip(local_reverse, remote_reverse)
    ]
    grad_proj = jnp.concatenate(
        [forward_parts[1], forward_parts[2], reverse_parts[1], reverse_parts[2]], axis=1
    ).astype(jnp.bfloat16)
    projected_back = lax.dot_general(
        grad_proj, all_weights, (((1,), (1,)), ((), ())), preferred_element_type=jnp.float32
    )
    grad_inputs = (forward_parts[0] + reverse_parts[0] + projected_back).astype(jnp.bfloat16)
    grad_weight = lax.psum_scatter(
        lax.dot_general(
            activations, grad_proj, (((0,), (0,)), ((), ())), preferred_element_type=jnp.float32
        ),
        ("dp", "seq"),
        scatter_dimension=0,
        tiled=True,
    )
    return (grad_inputs, grad_weight, forward_parts[3], reverse_parts[3])


def solution(mesh):
    placed = (
        P(("dp", "seq"), None),
        P(("dp", "seq"), None),
        P(("dp", "seq"), None),
        P(("dp", "seq"), None),
        P(("dp", "seq"), None),
        P(("dp", "seq"), None, None),
        P(("dp", "seq"), None, None),
    )
    return jax.shard_map(
        per_device,
        mesh=mesh,
        in_specs=placed,
        out_specs=(
            P(("dp", "seq"), None),
            P(("dp", "seq"), None),
            P(("dp", "seq"), None),
            P(("dp", "seq"), None),
        ),
        check_vma=False,
    )
```

profile of v0, /device:TPU:0, one launch (start us, length us, event | category | flops | bytes accessed | tf_op | source)
XLA Modules:
  0.0 591.3 jit_solution(4500699689343184046)
XLA Ops:
  7.2 73.5 %all_gather.23 = bf16[1280,256]{1,0:T(8,128)(2,1)S(1)} all-gather(bf16[40,256]{1,0:T(8,128)(2,1)} %param.17), channel_id=1, replica_groups=mesh['dp'=4,'seq'=8] {'dp','seq'}, dimensions={0}, use_global_device_ids=true | all-gather | bytes 675840 | tf_op jit(solution)/shard_map/all_gather | solution.py:152
  89.1 19.5 %rev.39 = bf16[512,1280]{1,0:T(8,128)(2,1)} reverse(bf16[512,1280]{1,0:T(8,128)(2,1)} %param.16), dimensions={0} | reverse | bytes 2621440 | tf_op jit(solution)/shard_map/rev | solution.py:159
  121.7 19.5 %rev.43 = bf16[512,1280]{1,0:T(8,128)(2,1)} reverse(bf16[512,1280]{1,0:T(8,128)(2,1)} %param.15), dimensions={0} | reverse | bytes 2621440 | tf_op jit(solution)/shard_map/rev | solution.py:158
  147.4 4.3 convolution_multiply_fusion
  161.7 75.9 %while.62 = (s32[]{:T(128)}, f32[5,512,4,64]{1,3,2,0:T(8,128)}, f32[5,512,512]{2,1,0:T(8,128)}, f32[5,4,512]{2,1,0:T(4,128)S(1)}, s32[5]{0:T(128)S(1)}, /*index=...) while((s32[]{:T(128)}, f32[5,512,4,64]{1,3,2,0:T(8,128)}, ...), condition=%wide.region_19.20_spmd.clone.clone, body=%wide.region_13.19_spmd.clone.clone.sunk | while | flops 283639872 | bytes 13814335 | solution.py:85
  164.4 4.8 fusion.141
  179.7 4.8 fusion.141
  194.9 4.8 fusion.141
  210.0 4.8 fusion.141
  225.2 4.8 fusion.141
  250.3 75.6 %while.61 = (s32[]{:T(128)}, f32[5,512,4,64]{1,3,2,0:T(8,128)}, f32[5,512,512]{2,1,0:T(8,128)}, f32[5,4,512]{2,1,0:T(4,128)S(1)}, s32[5]{0:T(128)S(1)}, /*index=...) while((s32[]{:T(128)}, f32[5,512,4,64]{1,3,2,0:T(8,128)}, ...), condition=%wide.region_8.9_spmd.clone.clone, body=%wide.region_2.8_spmd.clone.clone.sunk | while | flops 283639872 | bytes 13814335 | solution.py:85
  253.2 4.8 fusion.136
  268.3 4.8 fusion.136
  283.4 4.8 fusion.136
  298.4 4.8 fusion.136
  313.5 4.8 fusion.136
  342.8 16.3 %all-gather.3 = bf16[8,1,20]{2,1,0:T(2,128)(2,1)S(1)} all-gather(bf16[1,1,20]{2,1,0:T(2,128)(2,1)} %bitcast.232), channel_id=1, replica_groups=mesh['dp'=4,'seq'=8] {'seq'}, dimensions={0}, use_global_device_ids=true | all-gather | bytes 360 | tf_op jit(solution)/shard_map/all_gather | solution.py:26
  375.3 18.8 %all-gather.2 = f32[8,1,20]{2,1,0:T(1,128)} all-gather(f32[1,1,20]{2,1,0:T(1,128)S(1)} %bitcast.233), channel_id=1, replica_groups=mesh['dp'=4,'seq'=8] {'seq'}, dimensions={0}, use_global_device_ids=true | all-gather | bytes 720 | tf_op jit(solution)/shard_map/all_gather | solution.py:9
  410.4 16.7 %while.63 = (s32[]{:T(128)}, f32[64,1280]{1,0:T(8,128)S(1)}, s32[]{:T(128)}, f32[8,20]{1,0:T(8,128)}, f32[8,64,1280]{2,1,0:T(8,128)}, /*index=5*/s32[]{:T(128)}, s32[]{:T(128)}, s32[]{:T(128)}, s32[]{:T(128)}) while((s32[]{:T(128)}, f32[64,1280]{1,0:T(8,128)S(1)}, s32[]{:T(128)}, f32[8,20]{1,0:T(8,128)}, ...), condition=%wide.region_10.11_spmd.clone, body=%wide.region_9.10_spmd.clone.sunk | while | flops 327688 | bytes 1003927 | solution.py:20
  439.7 6.0 %fusion.55 = (f32[512,1280]{1,0:T(8,128)}, f32[512,1280]{1,0:T(8,128)}) fusion(f32[512,1280]{1,0:T(8,128)} %copy-done.6, bf16[512,1280]{1,0:T(8,128)(2,1)} %rev.43, f32[512,1280]{1,0:T(8,128)} %copy.130, bf16[512,64]{0,1:T(8,128)(2,1)} %copy-done.19, f32[64,1280]{1,0:T(8,128)S(1)} %get-tuple-element.297), kind=kOutput, calls=%fused_computation.76 | convolution fusion | flops 87244800 | bytes 12189696 | tf_op jit(solution)/shard_map/dot_general | solution.py:104
  454.2 20.8 %rev.44 = f32[512,1280]{1,0:T(8,128)} reverse(f32[512,1280]{1,0:T(8,128)} %get-tuple-element.513), dimensions={0} | reverse | bytes 5242880 | tf_op jit(solution)/shard_map/rev | solution.py:195
  475.0 4.2 fusion.53
  494.8 5.1 fusion.49
  499.9 84.8 %reduce-scatter.4.cloned.1.call-done = f32[40,256]{1,0:T(8,128)} async-done(((f32[1280,256]{1,0:T(8,128)}), f32[40,256]{1,0:T(8,128)}) %reduce-scatter.4.cloned.1.call-update) | async-done | bytes 40976
  (432 shorter events, 248.6 us)
Async XLA Ops:
  7.2 76.1 %copy-start.40 = (f32[512,20]{0,1:T(8,128)S(1)}, f32[512,20]{0,1:T(8,128)}, u32[]{:S(2)}) copy-start(f32[512,20]{0,1:T(8,128)} %param.19) | copy-start | bytes 122884
  7.2 391.1 %all-gather.9.cloned.1.call-start = ((), (), s32[]{:S(2)}) async-start(), calls=%async_computation.2 | async-start | bytes 1474560 | tf_op jit(solution)/shard_map/all_gather | solution.py:26
  80.8 6.2 %copy-start.11 = (bf16[1280,256]{1,0:T(8,128)(2,1)}, bf16[1280,256]{1,0:T(8,128)(2,1)S(1)}, u32[]{:S(2)}) copy-start(bf16[1280,256]{1,0:T(8,128)(2,1)S(1)} %all_gather.23) | copy-start | bytes 1966084
  82.9 58.3 %copy-start.17 = (bf16[512,256]{0,1:T(8,128)(2,1)}, bf16[512,256]{0,1:T(8,128)(2,1)S(1)}, u32[]{:S(2)}) copy-start(bf16[512,256]{0,1:T(8,128)(2,1)S(1)} %convolution_convert_fusion) | copy-start | bytes 786436
  89.1 21.9 %copy-start = (f32[512,1280]{1,0:T(8,128)}, f32[512,1280]{1,0:T(8,128)S(1)}, u32[]{:S(2)}) copy-start(f32[512,1280]{1,0:T(8,128)S(1)} %copy.128) | copy-start | bytes 7864324
  111.0 299.3 %all-gather.7.cloned.1.call-start = ((), (), s32[]{:S(2)}) async-start(), calls=%async_computation.1 | async-start | bytes 2949120 | tf_op jit(solution)/shard_map/all_gather | solution.py:9
  119.2 465.6 %reduce-scatter.4.cloned.1.call-start = ((), (), s32[]{:S(2)}) async-start(), calls=%async_computation.3 | async-start | bytes 1351680
  153.2 186.9 %copy-start.19 = (bf16[512,64]{0,1:T(8,128)(2,1)}, bf16[512,64]{0,1:T(8,128)(2,1)S(1)}, u32[]{:S(2)}) copy-start(bf16[512,64]{0,1:T(8,128)(2,1)S(1)} %rev.40) | copy-start | bytes 196612
  164.3 4.9 copy-start.4
  194.8 4.9 copy-start.4
  209.9 4.9 copy-start.4
  237.6 104.4 %copy-start.20 = (f32[512,20]{0,1:T(8,128)}, f32[512,20]{0,1:T(8,128)S(1)}, u32[]{:S(2)}) copy-start(f32[512,20]{0,1:T(8,128)S(1)} %get-tuple-element.847) | copy-start | bytes 122884
  250.3 75.6 %copy-start.14 = (bf16[1,64,1280]{2,1,0:T(8,128)(2,1)S(1)}, bf16[1,64,1280]{2,1,0:T(8,128)(2,1)}, u32[]{:S(2)}) copy-start(bf16[1,64,1280]{2,1,0:T(8,128)(2,1)} %param.20) | copy-start | bytes 491524
  359.7 5.4 copy-start.30
  371.0 23.8 %copy-start.15 = (bf16[1,64,1280]{2,1,0:T(8,128)(2,1)S(1)}, bf16[1,64,1280]{2,1,0:T(8,128)(2,1)}, u32[]{:S(2)}) copy-start(bf16[1,64,1280]{2,1,0:T(8,128)(2,1)} %param.20) | copy-start | bytes 491524
  375.1 21.5 %copy-start.7 = (bf16[512,512]{1,0:T(8,128)(2,1)S(1)}, bf16[512,512]{1,0:T(8,128)(2,1)}, u32[]{:S(2)}) copy-start(bf16[512,512]{1,0:T(8,128)(2,1)} %reduce_sum.148) | copy-start | bytes 1572868
  403.8 6.5 %copy-start.6 = (f32[512,1280]{1,0:T(8,128)}, f32[512,1280]{1,0:T(8,128)S(1)}, u32[]{:S(2)}) copy-start(f32[512,1280]{1,0:T(8,128)S(1)} %copy.129) | copy-start | bytes 7864324
  410.4 16.8 %copy-start.16 = (bf16[1,64,1280]{2,1,0:T(8,128)(2,1)S(1)}, bf16[1,64,1280]{2,1,0:T(8,128)(2,1)}, u32[]{:S(2)}) copy-start(bf16[1,64,1280]{2,1,0:T(8,128)(2,1)} %param.20) | copy-start | bytes 491524
  482.4 10.8 %copy-start.44 = (f32[20]{0:T(128)S(1)}, f32[20]{0:T(128)}, u32[]{:S(2)}) copy-start(f32[20]{0:T(128)} %get-tuple-element.454) | copy-start | bytes 244
  482.4 12.3 %copy-start.12 = (bf16[1280,256]{1,0:T(8,128)(2,1)S(1)}, bf16[1280,256]{1,0:T(8,128)(2,1)}, u32[]{:S(2)}) copy-start(bf16[1280,256]{1,0:T(8,128)(2,1)} %copy-done.11) | copy-start | bytes 1966084
  482.4 12.3 %copy-start.23 = (bf16[512,64]{0,1:T(8,128)(2,1)S(1)}, bf16[512,64]{0,1:T(8,128)(2,1)}, u32[]{:S(2)}) copy-start(bf16[512,64]{0,1:T(8,128)(2,1)} %multiply_convert_fusion) | copy-start | bytes 196612
  482.4 12.3 %copy-start.25 = (bf16[512,64]{0,1:T(8,128)(2,1)S(1)}, bf16[512,64]{0,1:T(8,128)(2,1)}, u32[]{:S(2)}) copy-start(bf16[512,64]{0,1:T(8,128)(2,1)} %fusion.65) | copy-start | bytes 196612
  482.5 12.3 %copy-start.27 = (bf16[512,64]{0,1:T(8,128)(2,1)S(1)}, bf16[512,64]{0,1:T(8,128)(2,1)}, u32[]{:S(2)}) copy-start(bf16[512,64]{0,1:T(8,128)(2,1)} %copy-done.26) | copy-start | bytes 196612
  482.5 12.3 %copy-start.29 = (bf16[512,64]{0,1:T(8,128)(2,1)S(1)}, bf16[512,64]{0,1:T(8,128)(2,1)}, u32[]{:S(2)}) copy-start(bf16[512,64]{0,1:T(8,128)(2,1)} %rev.45) | copy-start | bytes 196612
  (32 other events, 111.2 us)
Sparse Core Ops, SparseCore 0:
  111.2 38.6 all-gather.8
  152.1 53.3 all-gather.6
  439.8 144.8 reduce-scatter.3
where the time goes:
time: 601 us; the launch traced here: 591 us
  local copies, waits for them, and re-layouts  173 us (29%)
  matrix products  131 us (22%)
  blocking collectives  109 us (18%)
  waiting for transfers between devices  84.9 us (14%)
  other arithmetic  71.3 us (12%)
  between operations  14.4 us (2%)
  loops' own time  7.35 us (1%)
    unnamed x4, waiting for transfers between devices  84.9 us
    all_gather x1, blocking collectives, per_device(): all_weights = lax.all_gather(w_proj, ('dp', 'seq'), axis=0, tiled=True)  73.5 us
    dot_general x10, matrix products, one_group(): jnp.einsum('thp,uhp->htu', in_group, cot_group, preferred_element_type=jn...  48.1 us
    dot_general x10, matrix products, one_group(): jnp.einsum('htu,uhp->thp', weighted.astype(jnp.bfloat16), cot_group, pref...  36.3 us
    another operation x51, other arithmetic  26.4 us
    rev x3, local copies, waits for them, and re-layouts, per_device(): (near_term + far_term)[::-1]  25 us
    dynamic_update_slice x10, local copies, waits for them, and re-layouts, intra_terms(): lax.map(one_group, jnp.arange(head_count // group_size))  23 us
    rev x2, local copies, waits for them, and re-layouts, per_device(): flipped_cot = cotangent[::-1]  21.9 us
  transfers between devices with their start and end apart: 3, of which 1 were waited for; matrix products, arithmetic and copies ran while one was open for 53% of the time, Pallas kernels for 0%

commit v1 on v0

v1 whole, which is shorter than its diff:
```python
import functools

import jax
import jax.numpy as jnp
from jax import lax
from jax.experimental import pallas as pl
from jax.experimental.pallas import tpu as pltpu
from jax.sharding import PartitionSpec as P

F32, BF16 = jnp.float32, jnp.bfloat16
MESH = pl.DeviceIdType.MESH
LOG2E = 1.4426950408889634
TILE = 128
VMEM_LIMIT = 56 * 1024 * 1024


def mm(a, b, ca=1, cb=0):
    return lax.dot_general(a, b, (((ca,), (cb,)), ((), ())), preferred_element_type=F32)


def exact_mm(ones, x):
    hi = x.astype(BF16)
    rest = x - hi.astype(F32)
    mid = rest.astype(BF16)
    low = (rest - mid.astype(F32)).astype(BF16)
    return mm(ones, hi) + mm(ones, mid) + mm(ones, low)


def sum_mm(x, ones):
    hi = x.astype(BF16)
    low = (x - hi.astype(F32)).astype(BF16)
    return mm(hi, ones) + mm(low, ones)


def greet_all(n, n_seq, me):
    barrier = pltpu.get_barrier_semaphore()

    def greet(k, _):
        to = lax.rem(me + k, n)
        pl.semaphore_signal(barrier, inc=1, device_id=(to // n_seq, lax.rem(to, n_seq)), device_id_type=MESH)
        return 0

    lax.fori_loop(1, n, greet, 0)
    pl.semaphore_wait(barrier, n - 1)


def gather_kernel(n, n_seq, w_ref, out_ref, mine, recv, whole, ssem, rsem):
    me = lax.axis_index("dp") * n_seq + lax.axis_index("seq")
    rows = w_ref.shape[0]
    greet_all(n, n_seq, me)
    part = w_ref[...].astype(F32)
    half = part.shape[1] // 2
    mine[...] = jnp.concatenate([part[:, :half], part[:, half:]], axis=0).astype(BF16)

    def copy(k, slot):
        to = lax.rem(me + k, n)
        return pltpu.make_async_remote_copy(
            src_ref=mine, dst_ref=recv.at[slot], send_sem=ssem.at[k], recv_sem=rsem.at[slot],
            device_id=(to // n_seq, lax.rem(to, n_seq)), device_id_type=MESH)

    def send(k, _):
        copy(k, me).start()
        return 0

    lax.fori_loop(1, n, send, 0)

    def place(source, block):
        block = block.astype(F32)
        at = pl.ds(pl.multiple_of(source * rows, 8), rows)
        whole[at, :half] = block[:rows]
        whole[at, half:] = block[rows:]

    place(me, mine[...])

    def take(k, _):
        source = lax.rem(me + n - k, n)
        copy(k, source).wait_recv()
        place(source, recv[source])
        return 0

    lax.fori_loop(1, n, take, 0)
    out_ref[...] = whole[...].astype(BF16)

    def sent(k, _):
        copy(k, me).wait_send()
        return 0

    lax.fori_loop(1, n, sent, 0)


def scatter_kernel(n, n_seq, parts_ref, out_ref, recv, ssem, rsem):
    me = lax.axis_index("dp") * n_seq + lax.axis_index("seq")
    rows = out_ref.shape[0]
    half = out_ref.shape[1] // 2
    greet_all(n, n_seq, me)

    def copy(k, slot):
        to = lax.rem(me + k, n)
        return pltpu.make_async_remote_copy(
            src_ref=parts_ref.at[to], dst_ref=recv.at[slot], send_sem=ssem.at[k], recv_sem=rsem.at[slot],
            device_id=(to // n_seq, lax.rem(to, n_seq)), device_id_type=MESH)

    def send(k, _):
        copy(k, me).start()
        return 0

    lax.fori_loop(1, n, send, 0)

    def take(k, total):
        source = lax.rem(me + n - k, n)
        copy(k, source).wait_recv()
        return total + recv[source].astype(F32)

    total = lax.fori_loop(1, n, take, parts_ref[me].astype(F32))
    out_ref[:, :half] = total[:rows]
    out_ref[:, half:] = total[rows:]

    def sent(k, _):
        copy(k, me).wait_send()
        return 0

    lax.fori_loop(1, n, sent, 0)


def main_kernel(n_seq, heads, split,
                act, cot, w, fdec, rdec, fstate, rstate,
                gin_out, gw_out, gfd_out, grd_out,
                bcf, bcr, rowf, rowr, pad, proj, sc, macc, gx, incf, incr, colf, colr,
                msg, recv, carried, low, gbc, starts, carries, gwf, ssem, rsem):
    my_dp, me = lax.axis_index("dp"), lax.axis_index("seq")
    length, width = act.shape
    pairs = width // TILE
    state = w.shape[1] // 4
    scaling = state ** -0.5
    tiles = length // TILE
    barrier = pltpu.get_barrier_semaphore()

    def greet(k, _):
        pl.semaphore_signal(barrier, inc=1, device_id=(my_dp, lax.rem(me + k, n_seq)), device_id_type=MESH)
        return 0

    lax.fori_loop(1, n_seq, greet, 0)

    ti = lax.broadcasted_iota(jnp.int32, (length, length), 0)
    ui = lax.broadcasted_iota(jnp.int32, (length, length), 1)
    lower = jnp.where(ui <= ti, 1.0, 0.0).astype(BF16)
    upper = jnp.where(ui >= ti, 1.0, 0.0).astype(BF16)
    for dec, ones, bc, row in ((fdec, lower, bcf, rowf), (rdec, upper, bcr, rowr)):
        pad[...] = jnp.zeros_like(pad)
        pad[:, :heads] = dec[...]
        cum = exact_mm(ones, pad[...]) * LOG2E
        across = cum.T
        for h in range(heads):
            row[h] = jnp.broadcast_to(across[h:h + 1], (8, length))
            bc[h] = jnp.broadcast_to(cum[:, h:h + 1], (length, TILE))

    proj[...] = mm(act[...], w[...]).astype(BF16)
    bf, cf = proj[:, :state], proj[:, state:2 * state]
    br, cr = proj[:, 2 * state:3 * state], proj[:, 3 * state:]
    sf = scaling * mm(bf, cf, 1, 1)
    sr = scaling * mm(br, cr, 1, 1)
    sc[...] = jnp.where(ui > ti, sf, jnp.where(ui < ti, sr, sf + sr))

    lane = lax.broadcasted_iota(jnp.int32, (length, TILE), 1)
    first = lane < TILE // 2
    cft = cf.astype(F32).T.astype(BF16)
    crt = cr.astype(F32).T.astype(BF16)
    row16 = lax.broadcasted_iota(jnp.int32, (16, TILE), 0)

    def columns(p):
        return pl.ds(pl.multiple_of(p * TILE, TILE), TILE)

    def summary(p, _):
        c = cot[:, columns(p)].astype(F32)
        for d, (bc, ct, last) in enumerate(((bcf, cft, length - 1), (bcr, crt, 0))):
            g = jnp.exp2(jnp.where(first, bc[2 * p], bc[2 * p + 1]))
            out = scaling * mm(ct, (c * g).astype(BF16))
            f = g[last:last + 1]
            hi = f.astype(BF16).astype(F32)
            tail = jnp.where(row16 == 0, hi, jnp.where(row16 == 1, f - hi, 0.0))
            msg[d, :, columns(p)] = jnp.concatenate([out, tail], axis=0).astype(BF16)
        return 0

    lax.fori_loop(0, pairs, summary, 0)
    pl.semaphore_wait(barrier, n_seq - 1)

    def copy(k, slot):
        to = lax.rem(me + k, n_seq)
        return pltpu.make_async_remote_copy(
            src_ref=msg.at[jnp.where(to > me, 1, 0)], dst_ref=recv.at[slot],
            send_sem=ssem.at[k], recv_sem=rsem.at[slot],
            device_id=(my_dp, to), device_id_type=MESH)

    def send(k, _):
        copy(k, me).start()
        return 0

    lax.fori_loop(1, n_seq, send, 0)

    macc[...] = jnp.zeros_like(macc)
    incf[...] = jnp.zeros_like(incf)
    incr[...] = jnp.zeros_like(incr)
    tt = lax.broadcasted_iota(jnp.int32, (TILE, TILE), 0)
    uu = lax.broadcasted_iota(jnp.int32, (TILE, TILE), 1)
    tile_lane = uu
    half_row = lax.broadcasted_iota(jnp.int32, (1, TILE), 1) < TILE // 2
    masks = (jnp.where(half_row, 1.0, 0.0), jnp.where(half_row, 0.0, 1.0))

    def intra(p, _):
        a = act[:, columns(p)].astype(F32)
        c32 = cot[:, columns(p)].astype(F32)
        c = cot[:, columns(p)]
        am = [(a * m).astype(BF16) for m in masks]
        cm = [(c32 * m).astype(BF16) for m in masks]
        zero8 = jnp.zeros((8, TILE), F32)
        cols = [[[zero8] * tiles for _ in range(2)] for _ in range(2)]
        for i in range(tiles):
            rows = slice(i * TILE, (i + 1) * TILE)
            total = None
            mixes = [None] * tiles
            for j in range(2):
                h = 2 * p + j
                prod = mm(am[j][rows], c, 1, 1)
                fwd_t, rev_t = bcf[h, rows], bcr[h, rows]
                wl = []
                sums = [None, None]
                for q in range(tiles):
                    cs = slice(q * TILE, (q + 1) * TILE)
                    if q > i:
                        x = rowf[h, 0:1, cs] - fwd_t
                    elif q < i:
                        x = rowr[h, 0:1, cs] - rev_t
                    else:
                        x = jnp.where(uu >= tt, rowf[h, 0:1, cs] - fwd_t, rowr[h, 0:1, cs] - rev_t)
                    decay = jnp.exp2(x)
                    pt = prod[:, cs]
                    dp = decay * pt
                    mixes[q] = dp if mixes[q] is None else mixes[q] + dp
                    s = sc[rows, cs]
                    wl.append((s * decay).astype(BF16))
                    pair = s * dp
                    if q == i:
                        todo = ((0, jnp.where(uu > tt, pair, 0.0)), (1, jnp.where(uu < tt, pair, 0.0)))
                    else:
                        todo = ((0 if q > i else 1, pair),)
                    for d, term in todo:
                        sums[d] = term if sums[d] is None else sums[d] + term
                        cols[j][d][q] = cols[j][d][q] + term.reshape(TILE // 8, 8, TILE).sum(0)
                part = mm(jnp.concatenate(wl, axis=1), cm[j])
                total = part if total is None else total + part
                for d, inc in enumerate((incf, incr)):
                    summed = jnp.sum(sums[d], axis=1, keepdims=True)
                    inc[rows, :] = jnp.where(tile_lane == h, summed, inc[rows, :])
            gx[rows, columns(p)] = total
            for q in range(tiles):
                cs = slice(q * TILE, (q + 1) * TILE)
                macc[rows, cs] += mixes[q]
        for j in range(2):
            for d, col in enumerate((colf, colr)):
                col[2 * p + j] = jnp.concatenate(cols[j][d], axis=1)
        return 0

    lax.fori_loop(0, pairs, intra, 0)

    carried[...] = jnp.zeros_like(carried)

    def join(d, source):
        copy(lax.rem(me + n_seq - source, n_seq), source).wait_recv()
        tail = recv[source, state:, :].astype(F32)
        factor = tail[0:1] + tail[1:2]
        carried[d] = factor * carried[d] + recv[source, :state, :].astype(F32)

    def from_later(k, _):
        source = n_seq - 1 - k
        pl.when(source > me)(lambda: join(0, source))
        return 0

    def from_earlier(source, _):
        pl.when(source < me)(lambda: join(1, source))
        return 0

    lax.fori_loop(0, n_seq, from_later, 0)
    lax.fori_loop(0, n_seq, from_earlier, 0)
    low[...] = carried[...].astype(BF16)
    starts[...] = jnp.zeros_like(starts)
    carries[...] = jnp.zeros_like(carries)
    gbc[...] = jnp.zeros_like(gbc)
    sel_in = lax.broadcasted_iota(jnp.int32, (TILE, TILE), 0)
    sel_out = lax.broadcasted_iota(jnp.int32, (TILE, TILE), 1)

    def cross(p, wholes):
        a = act[:, columns(p)].astype(F32)
        c = cot[:, columns(p)].astype(F32)
        select = jnp.where(sel_out == 2 * p + sel_in // (TILE // 2), 1.0, 0.0).astype(BF16)
        out = []
        extra = gx[:, columns(p)]
        for d, (bc, init, b_rows, c_rows, last) in enumerate((
                (bcf, fstate, bf, cf, length - 1), (bcr, rstate, br, cr, 0))):
            cl = jnp.where(first, bc[2 * p], bc[2 * p + 1])
            end = cl[last:last + 1]
            shrink, growth = jnp.exp2(end - cl), jnp.exp2(cl)
            car, ini = low[d, :, columns(p)], init[:, columns(p)]
            b_car = mm(b_rows, car)
            c_ini = mm(c_rows, ini)
            extra = extra + shrink * b_car
            s_in, s_cot = a * shrink, c * growth
            gbc[2 * d] += mm(s_in.astype(BF16), car, 1, 1)
            gbc[2 * d + 1] += scaling * mm(s_cot.astype(BF16), ini, 1, 1)
            starts[d] += sum_mm(scaling * s_cot * c_ini, select)
            carries[d] += sum_mm(s_in * b_car, select)
            both = jnp.sum(car.astype(F32) * ini.astype(F32), axis=0, keepdims=True) * jnp.exp2(end)
            out.append(wholes[d] + sum_mm(jnp.broadcast_to(both, (8, TILE)), select))
        gx[:, columns(p)] = extra
        return tuple(out)

    wholes = lax.fori_loop(0, pairs, cross, (jnp.zeros((8, TILE), F32),) * 2)

    mix = macc[...]
    mixf = jnp.where(ui >= ti, mix, 0.0)
    mixr = jnp.where(ui <= ti, mix, 0.0)
    gbf = gbc[0] + scaling * mm(mixf.astype(BF16), cf)
    gcf = gbc[1] + scaling * mm(mixf.T.astype(BF16), bf)
    gbr = gbc[2] + scaling * mm(mixr.astype(BF16), cr)
    gcr = gbc[3] + scaling * mm(mixr.T.astype(BF16), br)
    gproj = jnp.concatenate([gbf, gcf, gbr, gcr], axis=1).astype(BF16)
    proj[...] = gproj

    def finish(p, _):
        gp = proj[...]
        wide = pl.ds(pl.multiple_of(p * 2 * TILE, 2 * TILE), 2 * TILE)
        gin_out[:, wide] = (gx[:, wide] + mm(gp, w[wide, :], 1, 1)).astype(BF16)
        gwf[wide, :] = mm(act[:, wide], gp, 0, 0)
        return 0

    lax.fori_loop(0, width // (2 * TILE), finish, 0)
    if split:
        count, rows = gw_out.shape[0], gw_out.shape[1] // 2

        def lay(k, _):
            at = pl.ds(pl.multiple_of(k * rows, 8), rows)
            gw_out[k] = jnp.concatenate([gwf[at, :TILE], gwf[at, TILE:]], axis=0).astype(BF16)
            return 0

        lax.fori_loop(0, count, lay, 0)
    else:
        gw_out[...] = gwf[...]

    below = jnp.where(ui < ti, 1.0, 0.0).astype(BF16)
    above = jnp.where(ui > ti, 1.0, 0.0).astype(BF16)
    for d, (inc, col, strict, incl, dest) in enumerate((
            (incf, colf, below, upper, gfd_out), (incr, colr, above, lower, grd_out))):
        by_head = jnp.concatenate([col[h].sum(0, keepdims=True) for h in range(heads)], axis=0)
        pad[...] = jnp.zeros_like(pad)
        pad[:, :heads] = by_head.T
        grad = exact_mm(strict, inc[...] - pad[...] + carries[d]) + exact_mm(incl, starts[d]) + wholes[d][0:1]
        dest[...] = grad[:, :heads]

    def sent(k, _):
        copy(k, me).wait_send()
        return 0

    lax.fori_loop(1, n_seq, sent, 0)


def per_device(n_dp, n_seq, activations, cotangent, w_proj, forward_decay, reverse_decay, forward_state, reverse_state):
    n = n_dp * n_seq
    length, width = activations.shape
    rows, columns = w_proj.shape
    heads = forward_decay.shape[1]
    state = columns // 4
    split = rows % 8 == 0
    in_vmem = pl.BlockSpec(memory_space=pltpu.VMEM)
    dma = pltpu.SemaphoreType.DMA
    if split:
        weights = pl.pallas_call(
            functools.partial(gather_kernel, n, n_seq),
            out_shape=jax.ShapeDtypeStruct((rows * n, columns), BF16),
            in_specs=[in_vmem], out_specs=in_vmem,
            scratch_shapes=[
                pltpu.VMEM((2 * rows, columns // 2), BF16),
                pltpu.VMEM((n, 2 * rows, columns // 2), BF16),
                pltpu.VMEM((rows * n, columns), F32),
                dma((n,)), dma((n,)),
            ],
            compiler_params=pltpu.CompilerParams(collective_id=0, has_side_effects=True, vmem_limit_bytes=VMEM_LIMIT),
        )(w_proj)
        gw_shape = jax.ShapeDtypeStruct((n, 2 * rows, columns // 2), BF16)
    else:
        weights = lax.all_gather(w_proj, ("dp", "seq"), axis=0, tiled=True)
        gw_shape = jax.ShapeDtypeStruct((width, columns), F32)
    big = lambda *shape: pltpu.VMEM(shape, F32)
    grad_inputs, gw_parts, grad_fwd, grad_rev = pl.pallas_call(
        functools.partial(main_kernel, n_seq, heads, split),
        out_shape=(
            jax.ShapeDtypeStruct((length, width), BF16), gw_shape,
            jax.ShapeDtypeStruct((length, heads), F32), jax.ShapeDtypeStruct((length, heads), F32)),
        in_specs=[in_vmem] * 7, out_specs=(in_vmem,) * 4,
        scratch_shapes=[
            big(heads, length, TILE), big(heads, length, TILE),
            big(heads, 8, length), big(heads, 8, length), big(length, TILE),
            pltpu.VMEM((length, columns), BF16),
            big(length, length), big(length, length), big(length, width),
            big(length, TILE), big(length, TILE), big(heads, 8, length), big(heads, 8, length),
            pltpu.VMEM((2, state + 16, width), BF16),
            pltpu.VMEM((n_seq, state + 16, width), BF16),
            big(2, state, width), pltpu.VMEM((2, state, width), BF16),
            big(4, length, state), big(2, length, TILE), big(2, length, TILE),
            big(width, columns),
            dma((n_seq,)), dma((n_seq,)),
        ],
        compiler_params=pltpu.CompilerParams(collective_id=1, has_side_effects=True, vmem_limit_bytes=VMEM_LIMIT),
    )(activations, cotangent, weights, forward_decay, reverse_decay, forward_state[0], reverse_state[0])
    if split:
        grad_weight = pl.pallas_call(
            functools.partial(scatter_kernel, n, n_seq),
            out_shape=jax.ShapeDtypeStruct((rows, columns), F32),
            in_specs=[in_vmem], out_specs=in_vmem,
            scratch_shapes=[pltpu.VMEM((n, 2 * rows, columns // 2), BF16), dma((n,)), dma((n,))],
            compiler_params=pltpu.CompilerParams(collective_id=2, has_side_effects=True, vmem_limit_bytes=VMEM_LIMIT),
        )(gw_parts)
    else:
        grad_weight = lax.psum_scatter(gw_parts, ("dp", "seq"), scatter_dimension=0, tiled=True)
    return grad_inputs, grad_weight, grad_fwd, grad_rev


def solution(mesh):
    rows, cube = P(("dp", "seq"), None), P(("dp", "seq"), None, None)
    return jax.shard_map(
        functools.partial(per_device, mesh.shape["dp"], mesh.shape["seq"]),
        mesh=mesh,
        in_specs=(rows,) * 5 + (cube,) * 2,
        out_specs=(rows,) * 4,
        check_vma=False,
    )
```

time: 601 us -> 116 us (0.19); the launches traced: 591 us -> 115 us
  local copies, waits for them, and re-layouts: 173 us -> 8.33 us
  matrix products: 131 us -> 0 us
  blocking collectives: 109 us -> 0 us
  Pallas kernels: 0 us -> 106 us
  waiting for transfers between devices: 84.9 us -> 0 us
  other arithmetic: 71.3 us -> 0 us
  between operations: 14.4 us -> 0.67 us
  loops' own time: 7.35 us -> 0 us
    dot_general x39 -> x0, matrix products: 131 us -> none  [the longest x10 48.1 us: one_group(): jnp.einsum('thp,uhp->htu', in_group, cot_group, preferred_element_type=jn...]
    all_gather x3 -> x0, blocking collectives: 109 us -> none  [the longest x1 73.5 us: per_device(): all_weights = lax.all_gather(w_proj, ('dp', 'seq'), axis=0, tiled=True)]
    pallas_call x0 -> x3, Pallas kernels: none -> 106 us  [the longest x1 49.9 us: per_device(): pl.pallas_call(functools.partial(main_kernel, n_seq, heads, split), out_s...]
    unnamed x4 -> x0, waiting for transfers between devices: 84.9 us -> none
    rev x12 -> x0, local copies, waits for them, and re-layouts: 72.7 us -> none  [the longest x3 25 us: per_device(): (near_term + far_term)[::-1]]
    another operation x51 -> x0, other arithmetic: 26.4 us -> none
    dynamic_update_slice x10 -> x0, local copies, waits for them, and re-layouts: 23 us -> none  [intra_terms(): lax.map(one_group, jnp.arange(head_count // group_size))]
    another operation x54 -> x0, local copies, waits for them, and re-layouts: 17 us -> none
  transfers between devices with their start and end apart: 3 -> 0, of which waited for: 1 -> 0; matrix products, arithmetic and copies ran while one was open for 53% -> 0% of each run, Pallas kernels for 0% -> 0%
where the time goes in v1:
time: 116 us; the launch traced here: 115 us
  Pallas kernels  106 us (91%)
  local copies, waits for them, and re-layouts  8.33 us (7%)
    pallas_call x1, Pallas kernels, per_device(): pl.pallas_call(functools.partial(main_kernel, n_seq, heads, split), out_s...  49.9 us
    pallas_call x1, Pallas kernels, per_device(): pl.pallas_call(functools.partial(scatter_kernel, n, n_seq), out_shape=jax...  32.5 us
    pallas_call x1, Pallas kernels, per_device(): pl.pallas_call(functools.partial(gather_kernel, n, n_seq), out_shape=jax....  23.9 us
    unnamed x10, local copies, waits for them, and re-layouts  8.33 us

profile of v1, /device:TPU:0, one launch (start us, length us, event | category | flops | bytes accessed | tf_op | source)
XLA Modules:
  0.0 115.3 jit_solution(16934901524513295056)
XLA Ops:
  0.6 1.6 %copy.11.fdec = f32[512,20]{1,0:T(8,128)} copy(f32[512,20]{0,1:T(8,128)} %param.10) | data formatting | bytes 81920 | tf_op args[3]
  2.3 1.6 %copy.12.rdec = f32[512,20]{1,0:T(8,128)} copy(f32[512,20]{0,1:T(8,128)} %param.11) | data formatting | bytes 81920 | tf_op args[4]
  3.9 23.9 %shard_map.102.w = bf16[1280,256]{1,0:T(8,128)(2,1)} custom-call(bf16[40,256]{1,0:T(8,128)(2,1)} %w_ref.1), custom_call_target="tpu_custom_call" | custom-call | tf_op jit(solution)/shard_map/pallas_call | solution.py:375
  27.8 49.9 %shard_map.103 = (bf16[512,1280]{1,0:T(8,128)(2,1)}, bf16[32,80,128]{2,1,0:T(8,128)(2,1)}, f32[512,20]{1,0:T(8,128)}, f32[512,20]{1,0:T(8,128)}) custom-call(bf16[512,1280]{1,0:T(8,128)(2,1)} %act.1, bf16[512,1280]{1,0:T(8,128)(2,1)} %cot.1, bf16[1280,256]{1,0:T(8,128)(2,1)} %shard_map.102.w, f32[512,20]{1,0:T(8,128)} %copy.11.fdec, f32[512,20]{1,0:T(8,128)} %copy.12.rdec, ...), custom_call_target="tpu_custom_call" | custom-call | tf_op jit(solution)/shard_map/pallas_call | solution.py:392
  77.7 0.0 copy-start
  77.7 32.5 %shard_map.104 = f32[40,256]{1,0:T(8,128)} custom-call(bf16[32,80,128]{2,1,0:T(8,128)(2,1)} %get-tuple-element.9.parts_ref), custom_call_target="tpu_custom_call" | custom-call | tf_op jit(solution)/shard_map/pallas_call | solution.py:414
  110.3 1.7 %copy.13 = f32[512,20]{0,1:T(8,128)} copy(f32[512,20]{1,0:T(8,128)} %get-tuple-element.14) | data formatting | bytes 81920
  111.9 1.7 %copy.14 = f32[512,20]{0,1:T(8,128)} copy(f32[512,20]{1,0:T(8,128)} %get-tuple-element.15) | data formatting | bytes 81920
  113.6 0.0 copy-done
  113.6 0.0 copy-start.1
  113.6 1.1 copy.17
  114.7 0.0 copy-done.1
  114.7 0.6 copy.18
Async XLA Ops:
  77.7 35.9 %copy-start = (bf16[512,1280]{1,0:T(8,128)(2,1)S(1)}, bf16[512,1280]{1,0:T(8,128)(2,1)}, u32[]{:S(2)}) copy-start(bf16[512,1280]{1,0:T(8,128)(2,1)} %get-tuple-element.20) | copy-start | bytes 3932164
  113.6 1.1 copy-start.1

commit v2 on v1

--- a/solution.py
+++ b/solution.py
@@ -18,12 +18,12 @@
     return lax.dot_general(a, b, (((ca,), (cb,)), ((), ())), preferred_element_type=F32)
 
 
-def exact_mm(ones, x):
+def exact_mm(x, ones):
     hi = x.astype(BF16)
     rest = x - hi.astype(F32)
     mid = rest.astype(BF16)
     low = (rest - mid.astype(F32)).astype(BF16)
-    return mm(ones, hi) + mm(ones, mid) + mm(ones, low)
+    return mm(hi, ones) + mm(mid, ones) + mm(low, ones)
 
 
 def sum_mm(x, ones):
@@ -32,105 +32,15 @@
     return mm(hi, ones) + mm(low, ones)
 
 
-def greet_all(n, n_seq, me):
-    barrier = pltpu.get_barrier_semaphore()
-
-    def greet(k, _):
-        to = lax.rem(me + k, n)
-        pl.semaphore_signal(barrier, inc=1, device_id=(to // n_seq, lax.rem(to, n_seq)), device_id_type=MESH)
-        return 0
-
-    lax.fori_loop(1, n, greet, 0)
-    pl.semaphore_wait(barrier, n - 1)
-
-
-def gather_kernel(n, n_seq, w_ref, out_ref, mine, recv, whole, ssem, rsem):
-    me = lax.axis_index("dp") * n_seq + lax.axis_index("seq")
-    rows = w_ref.shape[0]
-    greet_all(n, n_seq, me)
-    part = w_ref[...].astype(F32)
-    half = part.shape[1] // 2
-    mine[...] = jnp.concatenate([part[:, :half], part[:, half:]], axis=0).astype(BF16)
-
-    def copy(k, slot):
-        to = lax.rem(me + k, n)
-        return pltpu.make_async_remote_copy(
-            src_ref=mine, dst_ref=recv.at[slot], send_sem=ssem.at[k], recv_sem=rsem.at[slot],
-            device_id=(to // n_seq, lax.rem(to, n_seq)), device_id_type=MESH)
-
-    def send(k, _):
-        copy(k, me).start()
-        return 0
-
-    lax.fori_loop(1, n, send, 0)
-
-    def place(source, block):
-        block = block.astype(F32)
-        at = pl.ds(pl.multiple_of(source * rows, 8), rows)
-        whole[at, :half] = block[:rows]
-        whole[at, half:] = block[rows:]
-
-    place(me, mine[...])
-
-    def take(k, _):
-        source = lax.rem(me + n - k, n)
-        copy(k, source).wait_recv()
-        place(source, recv[source])
-        return 0
-
-    lax.fori_loop(1, n, take, 0)
-    out_ref[...] = whole[...].astype(BF16)
-
-    def sent(k, _):
-        copy(k, me).wait_send()
-        return 0
-
-    lax.fori_loop(1, n, sent, 0)
-
-
-def scatter_kernel(n, n_seq, parts_ref, out_ref, recv, ssem, rsem):
-    me = lax.axis_index("dp") * n_seq + lax.axis_index("seq")
-    rows = out_ref.shape[0]
-    half = out_ref.shape[1] // 2
-    greet_all(n, n_seq, me)
-
-    def copy(k, slot):
-        to = lax.rem(me + k, n)
-        return pltpu.make_async_remote_copy(
-            src_ref=parts_ref.at[to], dst_ref=recv.at[slot], send_sem=ssem.at[k], recv_sem=rsem.at[slot],
-            device_id=(to // n_seq, lax.rem(to, n_seq)), device_id_type=MESH)
-
-    def send(k, _):
-        copy(k, me).start()
-        return 0
-
-    lax.fori_loop(1, n, send, 0)
-
-    def take(k, total):
-        source = lax.rem(me + n - k, n)
-        copy(k, source).wait_recv()
-        return total + recv[source].astype(F32)
-
-    total = lax.fori_loop(1, n, take, parts_ref[me].astype(F32))
-    out_ref[:, :half] = total[:rows]
-    out_ref[:, half:] = total[rows:]
-
-    def sent(k, _):
-        copy(k, me).wait_send()
-        return 0
-
-    lax.fori_loop(1, n, sent, 0)
-
-
 def main_kernel(n_seq, heads, split,
-                act, cot, w, fdec, rdec, fstate, rstate,
+                act, cot, w_in, fdec, rdec, fstate, rstate,
                 gin_out, gw_out, gfd_out, grd_out,
                 bcf, bcr, rowf, rowr, pad, proj, sc, macc, gx, incf, incr, colf, colr,
-                msg, recv, carried, low, gbc, starts, carries, gwf, ssem, rsem):
+                msg, recv, carried, low, gbc, starts, carries, gwf, ssem, rsem, *more):
     my_dp, me = lax.axis_index("dp"), lax.axis_index("seq")
     length, width = act.shape
     pairs = width // TILE
-    state = w.shape[1] // 4
+    state = w_in.shape[1] // 4
     scaling = state ** -0.5
     tiles = length // TILE
     barrier = pltpu.get_barrier_semaphore()
@@ -140,20 +50,93 @@
         return 0
 
     lax.fori_loop(1, n_seq, greet, 0)
+    if split:
+        (w, wslots, w_ssem, w_rsem, parts, from_core, mid, from_x, last_parts, from_seq,
+         g_ssem, g_rsem) = more
+        core_row = my_dp + 1 - 2 * lax.rem(my_dp, 2)
+        x_row = lax.rem(my_dp + 2, 4)
+        far_row = lax.rem(core_row + 2, 4)
+        for other in (core_row, x_row):
+            pl.semaphore_signal(barrier, inc=1, device_id=(other, me), device_id_type=MESH)
+        pl.semaphore_wait(barrier, n_seq + 1)
+        w_rows = w_in.shape[0]
+        part = w_in[...].astype(F32)
+        own = my_dp * n_seq + me
+        wslots[own] = jnp.concatenate([part[:, :TILE], part[:, TILE:]], axis=0).astype(BF16)
+
+        def w_copy(slot, send, row, seq):
+            return pltpu.make_async_remote_copy(
+                src_ref=wslots.at[slot], dst_ref=wslots.at[slot], send_sem=w_ssem.at[send],
+                recv_sem=w_rsem.at[slot], device_id=(row, seq), device_id_type=MESH)
+
+        def w_first(k, _):
+            w_copy(own, k, my_dp, lax.rem(me + k, n_seq)).start()
+            return 0
+
+        def w_spread(s):
+            slot = my_dp * n_seq + s
+            w_copy(slot, n_seq + s, x_row, me).start()
+            w_copy(slot, 2 * n_seq + s, core_row, me).start()
+
+        def w_second(k, _):
+            s = lax.rem(me + n_seq - k, n_seq)
+            w_copy(my_dp * n_seq + s, 0, my_dp, me).wait_recv()
+            w_spread(s)
+            return 0
+
+        def w_third(k, _):
+            s = lax.rem(me + n_seq - k, n_seq)
+            slot = x_row * n_seq + s
+            w_copy(slot, 0, x_row, me).wait_recv()
+            w_copy(slot, 3 * n_seq + s, core_row, me).start()
+            return 0
+
+        def w_fourth(k, _):
+            s = lax.rem(me + n_seq - k, n_seq)
+            w_copy(core_row * n_seq + s, 0, core_row, me).wait_recv()
+            w_copy(far_row * n_seq + s, 0, core_row, me).wait_recv()
+            return 0
+
+        def w_place(d, _):
+            block = wslots[d].astype(F32)
+            at = pl.ds(pl.multiple_of(d * w_rows, 8), w_rows)
+            gwf[at, :TILE] = block[:w_rows]
+            gwf[at, TILE:] = block[w_rows:]
+            return 0
+
+        def w_sent(k, _):
+            pl.when(k > 0)(lambda: w_copy(own, k, my_dp, lax.rem(me + k, n_seq)).wait_send())
+            w_copy(my_dp * n_seq + k, n_seq + k, x_row, me).wait_send()
+            w_copy(my_dp * n_seq + k, 2 * n_seq + k, core_row, me).wait_send()
+            w_copy(x_row * n_seq + k, 3 * n_seq + k, core_row, me).wait_send()
+            return 0
+
+        lax.fori_loop(1, n_seq, w_first, 0)
+        w_spread(me)
+    else:
+        w = w_in
+        pl.semaphore_wait(barrier, n_seq - 1)
 
     ti = lax.broadcasted_iota(jnp.int32, (length, length), 0)
     ui = lax.broadcasted_iota(jnp.int32, (length, length), 1)
     lower = jnp.where(ui <= ti, 1.0, 0.0).astype(BF16)
     upper = jnp.where(ui >= ti, 1.0, 0.0).astype(BF16)
-    for dec, ones, bc, row in ((fdec, lower, bcf, rowf), (rdec, upper, bcr, rowr)):
-        pad[...] = jnp.zeros_like(pad)
-        pad[:, :heads] = dec[...]
-        cum = exact_mm(ones, pad[...]) * LOG2E
-        across = cum.T
+    if split:
+        lax.fori_loop(1, n_seq, w_second, 0)
+    pad[...] = jnp.zeros_like(pad)
+    for dec, ones, bc, row in ((fdec, upper, bcf, rowf), (rdec, lower, bcr, rowr)):
+        pad[:heads] = dec[...]
+        across = exact_mm(pad[...], ones) * LOG2E
+        cum = across.T
         for h in range(heads):
             row[h] = jnp.broadcast_to(across[h:h + 1], (8, length))
             bc[h] = jnp.broadcast_to(cum[:, h:h + 1], (length, TILE))
 
+    if split:
+        lax.fori_loop(0, n_seq, w_third, 0)
+        lax.fori_loop(0, n_seq, w_fourth, 0)
+        lax.fori_loop(0, n_seq * 4, w_place, 0)
+        w[...] = gwf[...].astype(BF16)
     proj[...] = mm(act[...], w[...]).astype(BF16)
     bf, cf = proj[:, :state], proj[:, state:2 * state]
     br, cr = proj[:, 2 * state:3 * state], proj[:, 3 * state:]
@@ -182,7 +165,6 @@
         return 0
 
     lax.fori_loop(0, pairs, summary, 0)
-    pl.semaphore_wait(barrier, n_seq - 1)
 
     def copy(k, slot):
         to = lax.rem(me + k, n_seq)
@@ -325,35 +307,103 @@
     gproj = jnp.concatenate([gbf, gcf, gbr, gcr], axis=1).astype(BF16)
     proj[...] = gproj
 
-    def finish(p, _):
-        gp = proj[...]
+    def weight_part(p, _):
         wide = pl.ds(pl.multiple_of(p * 2 * TILE, 2 * TILE), 2 * TILE)
-        gin_out[:, wide] = (gx[:, wide] + mm(gp, w[wide, :], 1, 1)).astype(BF16)
-        gwf[wide, :] = mm(act[:, wide], gp, 0, 0)
-        return 0
-
-    lax.fori_loop(0, width // (2 * TILE), finish, 0)
-    if split:
-        count, rows = gw_out.shape[0], gw_out.shape[1] // 2
-
-        def lay(k, _):
-            at = pl.ds(pl.multiple_of(k * rows, 8), rows)
-            gw_out[k] = jnp.concatenate([gwf[at, :TILE], gwf[at, TILE:]], axis=0).astype(BF16)
-            return 0
-
-        lax.fori_loop(0, count, lay, 0)
+        gwf[wide, :] = mm(act[:, wide], proj[...], 0, 0)
+        return 0
+
+    def input_part(p, _):
+        wide = pl.ds(pl.multiple_of(p * 2 * TILE, 2 * TILE), 2 * TILE)
+        gin_out[:, wide] = (gx[:, wide] + mm(proj[...], w[wide, :], 1, 1)).astype(BF16)
+        return 0
+
+    below = jnp.where(ui < ti, 1.0, 0.0).astype(BF16)
+    above = jnp.where(ui > ti, 1.0, 0.0).astype(BF16)
+
+    def decay_part(d, inc, col, strict, incl, dest):
+        pad[:heads] = jnp.concatenate([col[h].sum(0, keepdims=True) for h in range(heads)], axis=0)
+        grad = exact_mm((inc[...] + carries[d]).T - pad[...], strict) + exact_mm(starts[d].T, incl)
+        dest[...] = (grad + wholes[d].T[:, 0:1])[:heads]
+
+    wides = width // (2 * TILE)
+    lax.fori_loop(0, wides, weight_part, 0)
+    if split:
+        def lay(d, _):
+            at = pl.ds(pl.multiple_of(d * w_rows, 8), w_rows)
+            parts[d] = jnp.concatenate([gwf[at, :TILE], gwf[at, TILE:]], axis=0).astype(BF16)
+            return 0
+
+        lax.fori_loop(0, n_seq * 4, lay, 0)
+
+        def row_of(r):
+            return pl.ds(r * n_seq, n_seq)
+
+        def to_core(i, row):
+            return pltpu.make_async_remote_copy(
+                src_ref=parts.at[row_of(row)], dst_ref=from_core.at[i], send_sem=g_ssem.at[2 * n_seq + i],
+                recv_sem=g_rsem.at[2 * n_seq + i], device_id=(core_row, me), device_id_type=MESH)
+
+        def to_x(s):
+            return pltpu.make_async_remote_copy(
+                src_ref=mid.at[s], dst_ref=from_x.at[s], send_sem=g_ssem.at[s],
+                recv_sem=g_rsem.at[s], device_id=(x_row, me), device_id_type=MESH)
+
+        def to_seq(s, slot):
+            return pltpu.make_async_remote_copy(
+                src_ref=last_parts.at[s], dst_ref=from_seq.at[slot], send_sem=g_ssem.at[n_seq + s],
+                recv_sem=g_rsem.at[n_seq + slot], device_id=(my_dp, s), device_id_type=MESH)
+
+        to_core(0, far_row).start()
+        to_core(1, core_row).start()
+    decay_part(0, incf, colf, above, lower, gfd_out)
+    if split:
+        to_core(0, far_row).wait_recv()
+
+        def second(k, _):
+            s = lax.rem(me + k, n_seq)
+            mid[s] = (parts[x_row * n_seq + s].astype(F32) + from_core[0, s].astype(F32)).astype(BF16)
+            to_x(s).start()
+            return 0
+
+        lax.fori_loop(1, n_seq + 1, second, 0)
+    lax.fori_loop(0, wides, input_part, 0)
+    if split:
+        to_core(1, core_row).wait_recv()
+
+        def third_sum(s):
+            to_x(s).wait_recv()
+            return parts[my_dp * n_seq + s].astype(F32) + from_core[1, s].astype(F32) + from_x[s].astype(F32)
+
+        def third(k, _):
+            s = lax.rem(me + k, n_seq)
+            last_parts[s] = third_sum(s).astype(BF16)
+            to_seq(s, me).start()
+            return 0
+
+        lax.fori_loop(1, n_seq, third, 0)
+        own_sum = third_sum(me)
+    decay_part(1, incr, colr, below, upper, grd_out)
+    if split:
+        def fourth(k, total):
+            s = lax.rem(me + n_seq - k, n_seq)
+            to_seq(s, s).wait_recv()
+            return total + from_seq[s].astype(F32)
+
+        total = lax.fori_loop(1, n_seq, fourth, own_sum)
+        gw_out[:, :TILE] = total[:w_rows]
+        gw_out[:, TILE:] = total[w_rows:]
+        to_core(0, far_row).wait_send()
+        to_core(1, core_row).wait_send()
+
+        def all_sent(k, _):
+            to_x(k).wait_send()
+            pl.when(k != me)(lambda: to_seq(k, me).wait_send())
+            return 0
+
+        lax.fori_loop(0, n_seq, all_sent, 0)
+        lax.fori_loop(0, n_seq, w_sent, 0)
     else:
         gw_out[...] = gwf[...]
-
-    below = jnp.where(ui < ti, 1.0, 0.0).astype(BF16)
-    above = jnp.where(ui > ti, 1.0, 0.0).astype(BF16)
-    for d, (inc, col, strict, incl, dest) in enumerate((
-            (incf, colf, below, upper, gfd_out), (incr, colr, above, lower, grd_out))):
-        by_head = jnp.concatenate([col[h].sum(0, keepdims=True) for h in range(heads)], axis=0)
-        pad[...] = jnp.zeros_like(pad)
-        pad[:, :heads] = by_head.T
-        grad = exact_mm(strict, inc[...] - pad[...] + carries[d]) + exact_mm(incl, starts[d]) + wholes[d][0:1]
-        dest[...] = grad[:, :heads]
 
     def sent(k, _):
         copy(k, me).wait_send()
@@ -368,59 +418,47 @@
     rows, columns = w_proj.shape
     heads = forward_decay.shape[1]
     state = columns // 4
-    split = rows % 8 == 0
+    split = rows % 8 == 0 and n_dp == 4
     in_vmem = pl.BlockSpec(memory_space=pltpu.VMEM)
     dma = pltpu.SemaphoreType.DMA
-    if split:
-        weights = pl.pallas_call(
-            functools.partial(gather_kernel, n, n_seq),
-            out_shape=jax.ShapeDtypeStruct((rows * n, columns), BF16),
-            in_specs=[in_vmem], out_specs=in_vmem,
-            scratch_shapes=[
-                pltpu.VMEM((2 * rows, columns // 2), BF16),
-                pltpu.VMEM((n, 2 * rows, columns // 2), BF16),
-                pltpu.VMEM((rows * n, columns), F32),
-                dma((n,)), dma((n,)),
-            ],
-            compiler_params=pltpu.CompilerParams(collective_id=0, has_side_effects=True, vmem_limit_bytes=VMEM_LIMIT),
-        )(w_proj)
-        gw_shape = jax.ShapeDtypeStruct((n, 2 * rows, columns // 2), BF16)
+    low = lambda *shape: pltpu.VMEM(shape, BF16)
+    big = lambda *shape: pltpu.VMEM(shape, F32)
+    if split:
+        weights = w_proj
+        gw_shape = jax.ShapeDtypeStruct((rows, columns), F32)
+        chunks = lambda *lead: low(*lead, 2 * rows, columns // 2)
+        more = [
+            low(width, columns), chunks(n), dma((4 * n_seq,)), dma((n,)),
+            chunks(n), chunks(2, n_seq), chunks(n_seq), chunks(n_seq), chunks(n_seq), chunks(n_seq),
+            dma((2 * n_seq + 2,)), dma((2 * n_seq + 2,)),
+        ]
     else:
         weights = lax.all_gather(w_proj, ("dp", "seq"), axis=0, tiled=True)
         gw_shape = jax.ShapeDtypeStruct((width, columns), F32)
-    big = lambda *shape: pltpu.VMEM(shape, F32)
-    grad_inputs, gw_parts, grad_fwd, grad_rev = pl.pallas_call(
+        more = []
+    grad_inputs, grad_weight, grad_fwd, grad_rev = pl.pallas_call(
         functools.partial(main_kernel, n_seq, heads, split),
         out_shape=(
             jax.ShapeDtypeStruct((length, width), BF16), gw_shape,
-            jax.ShapeDtypeStruct((length, heads), F32), jax.ShapeDtypeStruct((length, heads), F32)),
+            jax.ShapeDtypeStruct((heads, length), F32), jax.ShapeDtypeStruct((heads, length), F32)),
         in_specs=[in_vmem] * 7, out_specs=(in_vmem,) * 4,
         scratch_shapes=[
             big(heads, length, TILE), big(heads, length, TILE),
-            big(heads, 8, length), big(heads, 8, length), big(length, TILE),
-            pltpu.VMEM((length, columns), BF16),
+            big(heads, 8, length), big(heads, 8, length), big(TILE, length),
+            low(length, columns),
             big(length, length), big(length, length), big(length, width),
             big(length, TILE), big(length, TILE), big(heads, 8, length), big(heads, 8, length),
-            pltpu.VMEM((2, state + 16, width), BF16),
-            pltpu.VMEM((n_seq, state + 16, width), BF16),
-            big(2, state, width), pltpu.VMEM((2, state, width), BF16),
+            low(2, state + 16, width), low(n_seq, state + 16, width),
+            big(2, state, width), low(2, state, width),
             big(4, length, state), big(2, length, TILE), big(2, length, TILE),
             big(width, columns),
             dma((n_seq,)), dma((n_seq,)),
-        ],
-        compiler_params=pltpu.CompilerParams(collective_id=1, has_side_effects=True, vmem_limit_bytes=VMEM_LIMIT),
-    )(activations, cotangent, weights, forward_decay, reverse_decay, forward_state[0], reverse_state[0])
-    if split:
-        grad_weight = pl.pallas_call(
-            functools.partial(scatter_kernel, n, n_seq),
-            out_shape=jax.ShapeDtypeStruct((rows, columns), F32),
-            in_specs=[in_vmem], out_specs=in_vmem,
-            scratch_shapes=[pltpu.VMEM((n, 2 * rows, columns // 2), BF16), dma((n,)), dma((n,))],
-            compiler_params=pltpu.CompilerParams(collective_id=2, has_side_effects=True, vmem_limit_bytes=VMEM_LIMIT),
-        )(gw_parts)
-    else:
-        grad_weight = lax.psum_scatter(gw_parts, ("dp", "seq"), scatter_dimension=0, tiled=True)
-    return grad_inputs, grad_weight, grad_fwd, grad_rev
+        ] + more,
+        compiler_params=pltpu.CompilerParams(collective_id=0, has_side_effects=True, vmem_limit_bytes=VMEM_LIMIT),
+    )(activations, cotangent, weights, forward_decay.T, reverse_decay.T, forward_state[0], reverse_state[0])
+    if not split:
+        grad_weight = lax.psum_scatter(grad_weight, ("dp", "seq"), scatter_dimension=0, tiled=True)
+    return grad_inputs, grad_weight, grad_fwd.T, grad_rev.T
 
 
 def solution(mesh):

time: 116 us -> 86.3 us (0.74)
  Pallas kernels: 106 us -> 81.1 us
  local copies, waits for them, and re-layouts: 8.33 us -> 4.36 us
    pallas_call x2 -> x0, Pallas kernels: 56.4 us -> none  [the longest x1 32.5 us: per_device(): pl.pallas_call(functools.partial(scatter_kernel, n, n_seq), out_shape=jax...]
    pallas_call x1, Pallas kernels: 49.9 us -> 81.1 us  [per_device(): pl.pallas_call(functools.partial(main_kernel, n_seq, heads, split), out_s...]
    unnamed x10, local copies, waits for them, and re-layouts: 8.33 us -> 4.36 us
where the time goes in v2:
time: 86.3 us; the launch traced here: 86.2 us
  Pallas kernels  81.1 us (94%)
  local copies, waits for them, and re-layouts  4.36 us (5%)
    pallas_call x1, Pallas kernels, per_device(): pl.pallas_call(functools.partial(main_kernel, n_seq, heads, split), out_s...  81.1 us
    unnamed x10, local copies, waits for them, and re-layouts  4.36 us

profile of v2, /device:TPU:0, one launch (start us, length us, event | category | flops | bytes accessed | tf_op | source)
XLA Modules:
  0.0 86.2 jit_solution(17917238462710456143)
XLA Ops:
  0.6 81.1 %shard_map.102 = (bf16[512,1280]{1,0:T(8,128)(2,1)}, f32[40,256]{1,0:T(8,128)}, f32[20,512]{1,0:T(8,128)}, f32[20,512]{1,0:T(8,128)}) custom-call(bf16[512,1280]{1,0:T(8,128)(2,1)} %act.1, bf16[512,1280]{1,0:T(8,128)(2,1)} %cot.1, bf16[40,256]{1,0:T(8,128)(2,1)} %w_in.1, f32[20,512]{1,0:T(8,128)} %bitcast.10, f32[20,512]{1,0:T(8,128)} %bitcast.11, ...), custom_call_target="tpu_custom_call" | custom-call | tf_op jit(solution)/shard_map/pallas_call | solution.py:439
  81.8 0.0 copy-start.2
  81.8 0.0 copy-start.1
  81.8 0.0 copy-start
  81.8 2.5 %copy.15 = bf16[512,1280]{1,0:T(8,128)(2,1)} copy(bf16[512,1280]{1,0:T(8,128)(2,1)} %get-tuple-element.16) | data formatting | bytes 2621440
  84.3 0.0 copy-done.2
  84.3 0.6 copy.16
  84.9 0.0 copy-done.1
  84.9 0.6 copy.17
  85.5 0.0 copy-done
  85.6 0.6 copy.18
Async XLA Ops:
  81.8 2.5 %copy-start.2 = (f32[40,256]{1,0:T(8,128)S(1)}, f32[40,256]{1,0:T(8,128)}, u32[]{:S(2)}) copy-start(f32[40,256]{1,0:T(8,128)} %get-tuple-element.17) | copy-start | bytes 122884
  81.8 3.1 %copy-start.1 = (f32[20,512]{1,0:T(8,128)S(1)}, f32[20,512]{1,0:T(8,128)}, u32[]{:S(2)}) copy-start(f32[20,512]{1,0:T(8,128)} %get-tuple-element.10) | copy-start | bytes 122884
  81.8 3.7 %copy-start = (f32[20,512]{1,0:T(8,128)S(1)}, f32[20,512]{1,0:T(8,128)}, u32[]{:S(2)}) copy-start(f32[20,512]{1,0:T(8,128)} %get-tuple-element.11) | copy-start | bytes 122884

commit v3 on v2

--- a/solution.py
+++ b/solution.py
@@ -36,7 +36,7 @@
                 act, cot, w_in, fdec, rdec, fstate, rstate,
                 gin_out, gw_out, gfd_out, grd_out,
                 bcf, bcr, rowf, rowr, pad, proj, sc, macc, gx, incf, incr, colf, colr,
-                msg, recv, carried, low, gbc, starts, carries, gwf, ssem, rsem, *more):
+                msg, recv, tails, tails_in, spread, carried, low, gbc, starts, carries, gwf, ssem, rsem, *more):
     my_dp, me = lax.axis_index("dp"), lax.axis_index("seq")
     length, width = act.shape
     pairs = width // TILE
@@ -124,10 +124,12 @@
     if split:
         lax.fori_loop(1, n_seq, w_second, 0)
     pad[...] = jnp.zeros_like(pad)
-    for dec, ones, bc, row in ((fdec, upper, bcf, rowf), (rdec, lower, bcr, rowr)):
+    ends = []
+    for dec, ones, bc, row, last in ((fdec, upper, bcf, rowf, length - 1), (rdec, lower, bcr, rowr, 0)):
         pad[:heads] = dec[...]
         across = exact_mm(pad[...], ones) * LOG2E
         cum = across.T
+        ends.append(jnp.exp2(cum[last:last + 1]))
         for h in range(heads):
             row[h] = jnp.broadcast_to(across[h:h + 1], (8, length))
             bc[h] = jnp.broadcast_to(cum[:, h:h + 1], (length, TILE))
@@ -149,19 +151,20 @@
     cft = cf.astype(F32).T.astype(BF16)
     crt = cr.astype(F32).T.astype(BF16)
     row16 = lax.broadcasted_iota(jnp.int32, (16, TILE), 0)
+    for d in range(2):
+        f = ends[d]
+        hi = f.astype(BF16).astype(F32)
+        tails[d] = jnp.where(row16 == 0, hi, jnp.where(row16 == 1, f - hi, 0.0)).astype(BF16)
 
     def columns(p):
         return pl.ds(pl.multiple_of(p * TILE, TILE), TILE)
 
     def summary(p, _):
         c = cot[:, columns(p)].astype(F32)
-        for d, (bc, ct, last) in enumerate(((bcf, cft, length - 1), (bcr, crt, 0))):
+        for d, (bc, ct) in enumerate(((bcf, cft), (bcr, crt))):
             g = jnp.exp2(jnp.where(first, bc[2 * p], bc[2 * p + 1]))
             out = scaling * mm(ct, (c * g).astype(BF16))
-            f = g[last:last + 1]
-            hi = f.astype(BF16).astype(F32)
-            tail = jnp.where(row16 == 0, hi, jnp.where(row16 == 1, f - hi, 0.0))
-            msg[d, :, columns(p)] = jnp.concatenate([out, tail], axis=0).astype(BF16)
+            msg[d, :, columns(p)] = out.astype(BF16)
         return 0
 
     lax.fori_loop(0, pairs, summary, 0)
@@ -173,7 +176,15 @@
             send_sem=ssem.at[k], recv_sem=rsem.at[slot],
             device_id=(my_dp, to), device_id_type=MESH)
 
+    def tail_copy(k, slot):
+        to = lax.rem(me + k, n_seq)
+        return pltpu.make_async_remote_copy(
+            src_ref=tails.at[jnp.where(to > me, 1, 0)], dst_ref=tails_in.at[slot],
+            send_sem=ssem.at[n_seq + k], recv_sem=rsem.at[n_seq + slot],
+            device_id=(my_dp, to), device_id_type=MESH)
+
     def send(k, _):
+        tail_copy(k, me).start()
         copy(k, me).start()
         return 0
 
@@ -245,12 +256,15 @@
     lax.fori_loop(0, pairs, intra, 0)
 
     carried[...] = jnp.zeros_like(carried)
+    from_head = lax.broadcasted_iota(jnp.int32, (TILE, width), 0)
+    to_column = lax.broadcasted_iota(jnp.int32, (TILE, width), 1)
+    spread[...] = jnp.where(to_column // (width // heads) == from_head, 1.0, 0.0).astype(BF16)
 
     def join(d, source):
+        tail_copy(lax.rem(me + n_seq - source, n_seq), source).wait_recv()
         copy(lax.rem(me + n_seq - source, n_seq), source).wait_recv()
-        tail = recv[source, state:, :].astype(F32)
-        factor = tail[0:1] + tail[1:2]
-        carried[d] = factor * carried[d] + recv[source, :state, :].astype(F32)
+        tail = mm(tails_in[source], spread[...])
+        carried[d] = (tail[0:1] + tail[1:2]) * carried[d] + recv[source].astype(F32)
 
     def from_later(k, _):
         source = n_seq - 1 - k
@@ -267,21 +281,22 @@
     starts[...] = jnp.zeros_like(starts)
     carries[...] = jnp.zeros_like(carries)
     gbc[...] = jnp.zeros_like(gbc)
-    sel_in = lax.broadcasted_iota(jnp.int32, (TILE, TILE), 0)
-    sel_out = lax.broadcasted_iota(jnp.int32, (TILE, TILE), 1)
+    sel_in = lax.broadcasted_iota(jnp.int32, (2 * TILE, TILE), 0)
+    sel_out = lax.broadcasted_iota(jnp.int32, (2 * TILE, TILE), 1)
 
     def cross(p, wholes):
-        a = act[:, columns(p)].astype(F32)
-        c = cot[:, columns(p)].astype(F32)
-        select = jnp.where(sel_out == 2 * p + sel_in // (TILE // 2), 1.0, 0.0).astype(BF16)
+        wide = pl.ds(pl.multiple_of(p * 2 * TILE, 2 * TILE), 2 * TILE)
+        a = act[:, wide].astype(F32)
+        c = cot[:, wide].astype(F32)
+        select = jnp.where(sel_out == 4 * p + sel_in // (TILE // 2), 1.0, 0.0).astype(BF16)
         out = []
-        extra = gx[:, columns(p)]
+        extra = gx[:, wide]
         for d, (bc, init, b_rows, c_rows, last) in enumerate((
                 (bcf, fstate, bf, cf, length - 1), (bcr, rstate, br, cr, 0))):
-            cl = jnp.where(first, bc[2 * p], bc[2 * p + 1])
+            cl = jnp.concatenate([jnp.where(first, bc[4 * p], bc[4 * p + 1]), jnp.where(first, bc[4 * p + 2], bc[4 * p + 3])], axis=1)
             end = cl[last:last + 1]
             shrink, growth = jnp.exp2(end - cl), jnp.exp2(cl)
-            car, ini = low[d, :, columns(p)], init[:, columns(p)]
+            car, ini = low[d, :, wide], init[:, wide]
             b_car = mm(b_rows, car)
             c_ini = mm(c_rows, ini)
             extra = extra + shrink * b_car
@@ -291,11 +306,11 @@
             starts[d] += sum_mm(scaling * s_cot * c_ini, select)
             carries[d] += sum_mm(s_in * b_car, select)
             both = jnp.sum(car.astype(F32) * ini.astype(F32), axis=0, keepdims=True) * jnp.exp2(end)
-            out.append(wholes[d] + sum_mm(jnp.broadcast_to(both, (8, TILE)), select))
-        gx[:, columns(p)] = extra
+            out.append(wholes[d] + sum_mm(jnp.broadcast_to(both, (8, 2 * TILE)), select))
+        gx[:, wide] = extra
         return tuple(out)
 
-    wholes = lax.fori_loop(0, pairs, cross, (jnp.zeros((8, TILE), F32),) * 2)
+    wholes = lax.fori_loop(0, pairs // 2, cross, (jnp.zeros((8, TILE), F32),) * 2)
 
     mix = macc[...]
     mixf = jnp.where(ui >= ti, mix, 0.0)
@@ -407,6 +422,7 @@
 
     def sent(k, _):
         copy(k, me).wait_send()
+        tail_copy(k, me).wait_send()
         return 0
 
     lax.fori_loop(1, n_seq, sent, 0)
@@ -448,11 +464,12 @@
             low(length, columns),
             big(length, length), big(length, length), big(length, width),
             big(length, TILE), big(length, TILE), big(heads, 8, length), big(heads, 8, length),
-            low(2, state + 16, width), low(n_seq, state + 16, width),
+            low(2, state, width), low(n_seq, state, width),
+            low(2, 16, TILE), low(n_seq, 16, TILE), low(TILE, width),
             big(2, state, width), low(2, state, width),
             big(4, length, state), big(2, length, TILE), big(2, length, TILE),
             big(width, columns),
-            dma((n_seq,)), dma((n_seq,)),
+            dma((2 * n_seq,)), dma((2 * n_seq,)),
         ] + more,
         compiler_params=pltpu.CompilerParams(collective_id=0, has_side_effects=True, vmem_limit_bytes=VMEM_LIMIT),
     )(activations, cotangent, weights, forward_decay.T, reverse_decay.T, forward_state[0], reverse_state[0])

time: 86.3 us -> 80.6 us (0.934)
  Pallas kernels: 81.1 us -> 75.4 us
    pallas_call x1, Pallas kernels: 81.1 us -> 75.4 us  [per_device(): pl.pallas_call(functools.partial(main_kernel, n_seq, heads, split), out_s...]
where the time goes in v3:
time: 80.6 us; the launch traced here: 80.4 us
  Pallas kernels  75.4 us (94%)
  local copies, waits for them, and re-layouts  4.36 us (5%)
    pallas_call x1, Pallas kernels, per_device(): pl.pallas_call(functools.partial(main_kernel, n_seq, heads, split), out_s...  75.4 us
    unnamed x10, local copies, waits for them, and re-layouts  4.36 us

profile of v3, /device:TPU:0, one launch (start us, length us, event | category | flops | bytes accessed | tf_op | source)
XLA Modules:
  0.0 80.4 jit_solution(1468609975243496425)
XLA Ops:
  0.6 75.4 %shard_map.102 = (bf16[512,1280]{1,0:T(8,128)(2,1)}, f32[40,256]{1,0:T(8,128)}, f32[20,512]{1,0:T(8,128)}, f32[20,512]{1,0:T(8,128)}) custom-call(bf16[512,1280]{1,0:T(8,128)(2,1)} %act.1, bf16[512,1280]{1,0:T(8,128)(2,1)} %cot.1, bf16[40,256]{1,0:T(8,128)(2,1)} %w_in.1, f32[20,512]{1,0:T(8,128)} %bitcast.10, f32[20,512]{1,0:T(8,128)} %bitcast.11, ...), custom_call_target="tpu_custom_call" | custom-call | tf_op jit(solution)/shard_map/pallas_call | solution.py:455
  76.0 0.0 copy-start.2
  76.0 0.0 copy-start.1
  76.0 0.0 copy-start
  76.0 2.5 %copy.15 = bf16[512,1280]{1,0:T(8,128)(2,1)} copy(bf16[512,1280]{1,0:T(8,128)(2,1)} %get-tuple-element.16) | data formatting | bytes 2621440
  78.5 0.0 copy-done.2
  78.5 0.6 copy.16
  79.1 0.0 copy-done.1
  79.1 0.6 copy.17
  79.8 0.0 copy-done
  79.8 0.6 copy.18
Async XLA Ops:
  76.0 2.5 %copy-start.2 = (f32[40,256]{1,0:T(8,128)S(1)}, f32[40,256]{1,0:T(8,128)}, u32[]{:S(2)}) copy-start(f32[40,256]{1,0:T(8,128)} %get-tuple-element.17) | copy-start | bytes 122884
  76.0 3.1 %copy-start.1 = (f32[20,512]{1,0:T(8,128)S(1)}, f32[20,512]{1,0:T(8,128)}, u32[]{:S(2)}) copy-start(f32[20,512]{1,0:T(8,128)} %get-tuple-element.10) | copy-start | bytes 122884
  76.0 3.7 %copy-start = (f32[20,512]{1,0:T(8,128)S(1)}, f32[20,512]{1,0:T(8,128)}, u32[]{:S(2)}) copy-start(f32[20,512]{1,0:T(8,128)} %get-tuple-element.11) | copy-start | bytes 122884
